TPU v7x, 32 devices: a whole 2x2x4 slice. The times are simulated.
32 devices in a mesh: dp: 8 (over z, y), tensor: 4 (over x, core).
Axes of the slice: x: 2, y: 2, z: 4, core: 2. Of those that a mesh axis runs over, the one named last changes fastest.
Arguments:
- tokens: bfloat16 [8192, 768], P(('dp', 'tensor')), may hold values from -6 to 6
- lengths: int32 [8, 2], P('dp'), may hold values from 256 to 768, as said below
- w_qkv: bfloat16 [768, 3, 768], P('dp', None, 'tensor'), may hold values from -0.21875 to 0.21875
- w_attn_out: bfloat16 [768, 768], P('tensor', 'dp'), may hold values from -0.625 to 0.625
- w_in: bfloat16 [768, 2, 1152], P('dp', None, 'tensor'), may hold values from -0.21875 to 0.21875
- w_mlp_out: bfloat16 [1152, 768], P('tensor', 'dp'), may hold values from -0.1875 to 0.1875
- gain_attn: bfloat16 [768], P('dp'), may hold values from 0.5 to 1.5
- gain_mlp: bfloat16 [768], P('dp'), may hold values from 0.5 to 1.5
- cotangent: bfloat16 [8192, 768], P(('dp', 'tensor')), may hold values from -6 to 6
Outputs:
- output: bfloat16 [8192, 768], P(('dp', 'tensor'))
- grad_tokens: bfloat16 [8192, 768], P(('dp', 'tensor'))
- grad_qkv: float32 [768, 3, 768], P('dp', None, 'tensor')
- grad_attn_out: float32 [768, 768], P('tensor', 'dp')
- grad_in: float32 [768, 2, 1152], P('dp', None, 'tensor')
- grad_mlp_out: float32 [1152, 768], P('tensor', 'dp')
- grad_gain_attn: float32 [768], P('dp')
- grad_gain_mlp: float32 [768], P('dp')
Inputs may be any that keep to these rules, and one draw needn't show every extreme that they name: Each row gives the lengths of the two sequences packed in order at the start of one group's 1024 slots; their sum lies above 768 and at most 1024, and in every draw some group's two lengths are 256 and 768.
All inputs are finite; a program needn't handle non-finite values.
Results may differ from a plain program's by a relative error of at most 0.02.
Values may be sent and summed in bfloat16 or wider, within the bound.
A program may use at most 128 MiB of HBM per device.

v0:
```python
import jax
import jax.numpy as jnp
from jax import lax
from jax.sharding import PartitionSpec as P

HEAD_DIM = 64
WINDOW = 128


NORM_EPS = 1e-05
ROPE_BASE = 10000.0
MASKED = -1e30


def norm_rows(values, gain):
    centre = values - jnp.mean(values, axis=-1, keepdims=True)
    spread = jnp.mean(centre * centre, axis=-1, keepdims=True)
    return centre * lax.rsqrt(spread + NORM_EPS) * gain


def run_layout(seq_pair, slot_count):
    slot_ids = jnp.arange(slot_count, dtype=jnp.int32)
    first_end = seq_pair[0]
    second_end = seq_pair[0] + seq_pair[1]
    run_ids = (slot_ids >= first_end).astype(jnp.int32) + (slot_ids >= second_end).astype(jnp.int32)
    run_start = jnp.where(run_ids == 0, 0, jnp.where(run_ids == 1, first_end, second_end))
    return (run_ids, slot_ids - run_start)


def rope_tables(position, head_dim):
    half_dim = head_dim // 2
    inv_freq = ROPE_BASE ** (-(jnp.arange(half_dim, dtype=jnp.float32) * 2.0) / head_dim)
    angles = position.astype(jnp.float32)[:, None] * inv_freq[None, :]
    return (jnp.cos(angles)[:, None, :], jnp.sin(angles)[:, None, :])


def rotate(values, cos_tab, sin_tab):
    half_dim = values.shape[-1] // 2
    front_half = values[..., :half_dim]
    back_half = values[..., half_dim:]
    return jnp.concatenate(
        [front_half * cos_tab - back_half * sin_tab, back_half * cos_tab + front_half * sin_tab],
        axis=-1,
    )


def unrotate(values, cos_tab, sin_tab):
    half_dim = values.shape[-1] // 2
    front_half = values[..., :half_dim]
    back_half = values[..., half_dim:]
    return jnp.concatenate(
        [front_half * cos_tab + back_half * sin_tab, back_half * cos_tab - front_half * sin_tab],
        axis=-1,
    )


def window_allowed(run_ids, run_pad, first_row, block_rows, half_win):
    row_runs = lax.dynamic_slice_in_dim(run_ids, first_row, block_rows, 0)
    key_runs = lax.dynamic_slice_in_dim(run_pad, first_row, block_rows + 2 * half_win, 0)
    offsets = (
        jnp.arange(block_rows, dtype=jnp.int32)[:, None]
        + half_win
        - jnp.arange(block_rows + 2 * half_win, dtype=jnp.int32)[None, :]
    )
    return (row_runs[:, None] == key_runs[None, :]) & (jnp.abs(offsets) <= half_win)


def padded_inputs(key_rot, value_low, run_ids, half_win):
    key_pad = jnp.pad(key_rot, ((half_win, half_win), (0, 0), (0, 0)))
    value_pad = jnp.pad(value_low, ((half_win, half_win), (0, 0), (0, 0)))
    run_pad = jnp.pad(run_ids, (half_win, half_win), constant_values=-1)
    return (key_pad, value_pad, run_pad)


def block_scores(q_blk, k_blk, allowed, score_scale):
    scores = (
        jnp.einsum("ihc,jhc->hij", q_blk, k_blk, preferred_element_type=jnp.float32) * score_scale
    )
    return jnp.where(allowed[None], scores, MASKED)


def attend_forward(query_rot, key_rot, value_low, run_ids):
    slot_count, heads_here, head_dim = query_rot.shape
    block_rows = min(512, slot_count)
    half_win = WINDOW // 2
    key_width = block_rows + 2 * half_win
    score_scale = head_dim ** (-0.5)
    key_pad, value_pad, run_pad = padded_inputs(key_rot, value_low, run_ids, half_win)

    def one_block(block_index):
        first_row = block_index * block_rows
        q_blk = lax.dynamic_slice_in_dim(query_rot, first_row, block_rows, 0)
        k_blk = lax.dynamic_slice_in_dim(key_pad, first_row, key_width, 0)
        v_blk = lax.dynamic_slice_in_dim(value_pad, first_row, key_width, 0)
        allowed = window_allowed(run_ids, run_pad, first_row, block_rows, half_win)
        scores = block_scores(q_blk, k_blk, allowed, score_scale)
        row_max = jnp.max(scores, axis=-1, keepdims=True)
        exp_total = jnp.sum(jnp.exp(scores - row_max), axis=-1, keepdims=True)
        log_total = row_max + jnp.log(exp_total)
        attn_prob = jnp.exp(scores - log_total).astype(jnp.bfloat16)
        block_out = jnp.einsum("hij,jhc->ihc", attn_prob, v_blk, preferred_element_type=jnp.float32)
        return (block_out.astype(jnp.bfloat16), log_total)

    block_outs, log_totals = lax.map(
        one_block, jnp.arange(slot_count // block_rows, dtype=jnp.int32)
    )
    return (block_outs.reshape(slot_count, heads_here, head_dim), log_totals)


def attend_backward(query_rot, key_rot, value_low, run_ids, log_totals, grad_attended):
    slot_count, heads_here, head_dim = query_rot.shape
    block_rows = min(512, slot_count)
    half_win = WINDOW // 2
    key_width = block_rows + 2 * half_win
    score_scale = head_dim ** (-0.5)
    key_pad, value_pad, run_pad = padded_inputs(key_rot, value_low, run_ids, half_win)

    def one_block(carry, inputs):
        grad_key_pad, grad_value_pad = carry
        block_index, log_total = inputs
        first_row = block_index * block_rows
        q_blk = lax.dynamic_slice_in_dim(query_rot, first_row, block_rows, 0)
        k_blk = lax.dynamic_slice_in_dim(key_pad, first_row, key_width, 0)
        v_blk = lax.dynamic_slice_in_dim(value_pad, first_row, key_width, 0)
        g_blk = lax.dynamic_slice_in_dim(grad_attended, first_row, block_rows, 0)
        allowed = window_allowed(run_ids, run_pad, first_row, block_rows, half_win)
        scores = block_scores(q_blk, k_blk, allowed, score_scale)
        attn_prob = jnp.exp(scores - log_total)
        prob_low = attn_prob.astype(jnp.bfloat16)
        grad_v = jnp.einsum("hij,ihc->jhc", prob_low, g_blk, preferred_element_type=jnp.float32)
        grad_p = jnp.einsum("ihc,jhc->hij", g_blk, v_blk, preferred_element_type=jnp.float32)
        row_inner = jnp.sum(attn_prob * grad_p, axis=-1, keepdims=True)
        grad_s = (attn_prob * (grad_p - row_inner)).astype(jnp.bfloat16)
        grad_q = (
            jnp.einsum("hij,jhc->ihc", grad_s, k_blk, preferred_element_type=jnp.float32)
            * score_scale
        )
        grad_k = (
            jnp.einsum("hij,ihc->jhc", grad_s, q_blk, preferred_element_type=jnp.float32)
            * score_scale
        )
        key_part = lax.dynamic_slice_in_dim(grad_key_pad, first_row, key_width, 0) + grad_k
        value_part = lax.dynamic_slice_in_dim(grad_value_pad, first_row, key_width, 0) + grad_v
        grad_key_pad = lax.dynamic_update_slice_in_dim(grad_key_pad, key_part, first_row, 0)
        grad_value_pad = lax.dynamic_update_slice_in_dim(grad_value_pad, value_part, first_row, 0)
        return ((grad_key_pad, grad_value_pad), grad_q)

    zero_grads = jnp.zeros((slot_count + 2 * half_win, heads_here, head_dim), jnp.float32)
    block_ids = jnp.arange(slot_count // block_rows, dtype=jnp.int32)
    (grad_key_pad, grad_value_pad), grad_query = lax.scan(
        one_block, (zero_grads, zero_grads), (block_ids, log_totals)
    )
    grad_query = grad_query.reshape(slot_count, heads_here, head_dim)
    return (
        grad_query,
        grad_key_pad[half_win : half_win + slot_count],
        grad_value_pad[half_win : half_win + slot_count],
    )


def gated_unit(mixed_proj):
    return jax.nn.gelu(mixed_proj[:, 0], approximate=False) * mixed_proj[:, 1]


def on_device(tokens, lengths, w_qkv, w_attn_out, w_in, w_mlp_out, gain_attn, gain_mlp, cotangent):
    gathered = (
        lax.all_gather(w_qkv, "dp", axis=0, tiled=True),
        lax.all_gather(w_attn_out, "dp", axis=1, tiled=True),
        lax.all_gather(w_in, "dp", axis=0, tiled=True),
        lax.all_gather(w_mlp_out, "dp", axis=1, tiled=True),
        lax.all_gather(gain_attn, "dp", axis=0, tiled=True),
        lax.all_gather(gain_mlp, "dp", axis=0, tiled=True),
    )
    qkv_full, attn_out_full, in_full, mlp_out_full, gain_one, gain_two = gathered
    row_count = tokens.shape[0]
    slot_count = row_count * lax.axis_size("tensor")
    heads_here = qkv_full.shape[2] // HEAD_DIM
    run_ids, position = run_layout(lengths[0], slot_count)
    cos_tab, sin_tab = rope_tables(position, HEAD_DIM)
    tokens_f = tokens.astype(jnp.float32)
    normed_one_f, pull_norm_one = jax.vjp(norm_rows, tokens_f, gain_one.astype(jnp.float32))
    normed_one_full = lax.all_gather(
        normed_one_f.astype(jnp.bfloat16), "tensor", axis=0, tiled=True
    )
    proj = jnp.einsum("rd,dtc->rtc", normed_one_full, qkv_full, preferred_element_type=jnp.float32)
    proj = proj.reshape(slot_count, 3, heads_here, HEAD_DIM)
    query_rot = rotate(proj[:, 0], cos_tab, sin_tab).astype(jnp.bfloat16)
    key_rot = rotate(proj[:, 1], cos_tab, sin_tab).astype(jnp.bfloat16)
    value_low = proj[:, 2].astype(jnp.bfloat16)
    attended, log_totals = attend_forward(query_rot, key_rot, value_low, run_ids)
    attended_flat = attended.reshape(slot_count, heads_here * HEAD_DIM)
    rows_part = attended_flat
    hidden = tokens_f + lax.psum_scatter(
        jnp.dot(rows_part, attn_out_full, preferred_element_type=jnp.float32).astype(jnp.bfloat16),
        "tensor",
        scatter_dimension=0,
        tiled=True,
    ).astype(jnp.float32)
    normed_two_f, pull_norm_two = jax.vjp(norm_rows, hidden, gain_two.astype(jnp.float32))
    normed_two_full = lax.all_gather(
        normed_two_f.astype(jnp.bfloat16), "tensor", axis=0, tiled=True
    )
    mixed_proj = jnp.einsum(
        "rd,dtc->rtc", normed_two_full, in_full, preferred_element_type=jnp.float32
    )
    gated_f, pull_gate = jax.vjp(gated_unit, mixed_proj)
    gated_act = gated_f.astype(jnp.bfloat16)
    rows_part = gated_act
    output = (
        hidden
        + lax.psum_scatter(
            jnp.dot(rows_part, mlp_out_full, preferred_element_type=jnp.float32).astype(
                jnp.bfloat16
            ),
            "tensor",
            scatter_dimension=0,
            tiled=True,
        ).astype(jnp.float32)
    ).astype(jnp.bfloat16)
    grad_out_full = lax.all_gather(cotangent, "tensor", axis=0, tiled=True)
    grad_gated = jnp.einsum(
        "rd,fd->rf", grad_out_full, mlp_out_full, preferred_element_type=jnp.float32
    )
    grad_mlp_out_w = jnp.einsum(
        "rf,rd->fd", gated_act, grad_out_full, preferred_element_type=jnp.float32
    )
    grad_mixed = pull_gate(grad_gated)[0].astype(jnp.bfloat16)
    grad_in_w = jnp.einsum(
        "rd,rtc->dtc", normed_two_full, grad_mixed, preferred_element_type=jnp.float32
    )
    rows_part = grad_mixed
    grad_normed_two = lax.psum_scatter(
        jnp.einsum("rtc,dtc->rd", rows_part, in_full, preferred_element_type=jnp.float32).astype(
            jnp.bfloat16
        ),
        "tensor",
        scatter_dimension=0,
        tiled=True,
    ).astype(jnp.float32)
    grad_hidden_part, grad_gain_two = pull_norm_two(grad_normed_two)
    grad_hidden = cotangent.astype(jnp.float32) + grad_hidden_part
    grad_branch_full = lax.all_gather(
        grad_hidden.astype(jnp.bfloat16), "tensor", axis=0, tiled=True
    )
    grad_attn_out_w = jnp.einsum(
        "rc,rd->cd", attended_flat, grad_branch_full, preferred_element_type=jnp.float32
    )
    grad_attended = jnp.einsum(
        "rd,cd->rc", grad_branch_full, attn_out_full, preferred_element_type=jnp.float32
    )
    grad_attended = grad_attended.astype(jnp.bfloat16).reshape(slot_count, heads_here, HEAD_DIM)
    grad_query, grad_key, grad_value = attend_backward(
        query_rot, key_rot, value_low, run_ids, log_totals, grad_attended
    )
    grad_proj = jnp.stack(
        [unrotate(grad_query, cos_tab, sin_tab), unrotate(grad_key, cos_tab, sin_tab), grad_value],
        axis=1,
    )
    grad_proj = grad_proj.astype(jnp.bfloat16).reshape(slot_count, 3, heads_here * HEAD_DIM)
    grad_qkv_w = jnp.einsum(
        "rd,rtc->dtc", normed_one_full, grad_proj, preferred_element_type=jnp.float32
    )
    rows_part = grad_proj
    grad_normed_one = lax.psum_scatter(
        jnp.einsum("rtc,dtc->rd", rows_part, qkv_full, preferred_element_type=jnp.float32).astype(
            jnp.bfloat16
        ),
        "tensor",
        scatter_dimension=0,
        tiled=True,
    ).astype(jnp.float32)
    grad_rows_part, grad_gain_one = pull_norm_one(grad_normed_one)
    grad_tokens = (grad_hidden + grad_rows_part).astype(jnp.bfloat16)
    gain_sums = lax.psum((grad_gain_one, grad_gain_two), "tensor")
    results = (
        lax.psum_scatter(grad_qkv_w, "dp", scatter_dimension=0, tiled=True),
        lax.psum_scatter(grad_attn_out_w, "dp", scatter_dimension=1, tiled=True),
        lax.psum_scatter(grad_in_w, "dp", scatter_dimension=0, tiled=True),
        lax.psum_scatter(grad_mlp_out_w, "dp", scatter_dimension=1, tiled=True),
        lax.psum_scatter(gain_sums[0], "dp", scatter_dimension=0, tiled=True),
        lax.psum_scatter(gain_sums[1], "dp", scatter_dimension=0, tiled=True),
    )
    return (
        output,
        grad_tokens,
        results[0],
        results[1],
        results[2],
        results[3],
        results[4],
        results[5],
    )


def solution(mesh):
    return jax.shard_map(
        on_device,
        mesh=mesh,
        in_specs=(
            P(("dp", "tensor"), None),
            P("dp", None),
            P("dp", None, "tensor"),
            P("tensor", "dp"),
            P("dp", None, "tensor"),
            P("tensor", "dp"),
            P("dp"),
            P("dp"),
            P(("dp", "tensor"), None),
        ),
        out_specs=(
            P(("dp", "tensor"), None),
            P(("dp", "tensor"), None),
            P("dp", None, "tensor"),
            P("tensor", "dp"),
            P("dp", None, "tensor"),
            P("tensor", "dp"),
            P("dp"),
            P("dp"),
        ),
        check_vma=False,
    )
```

profile of v0, /device:TPU:8, one launch (start us, length us, event | category | flops | bytes accessed | tf_op | source)
XLA Modules:
  0.0 642.2 jit_solution(5594088659501147330)
XLA Ops:
  13.4 18.9 %all-reduce.11 = (bf16[768]{0:T(1024)(128)(2,1)S(1)}, bf16[768]{0:T(1024)(128)(2,1)S(1)}) all-reduce(bf16[768]{0:T(1024)(128)(2,1)S(1)} %dynamic-update-slice, bf16[768]{0:T(1024)(128)(2,1)S(1)} %dynamic-update-slice.1), channel_id=1, replica_groups=mesh['dp'=8,'tensor'=4] {'dp'}, use_global_device_ids=true, to_apply=%add.5 | all-reduce | flops 1536 | bytes 6144
  34.6 35.2 %all_gather.32 = bf16[768,3,192]{2,1,0:T(4,128)(2,1)S(1)} all-gather(bf16[96,3,192]{2,1,0:T(4,128)(2,1)S(1)} %copy.33), channel_id=1, replica_groups=mesh['dp'=8,'tensor'=4] {'dp'}, dimensions={0}, use_global_device_ids=true | all-gather | bytes 995328 | tf_op jit(solution)/shard_map/all_gather | solution.py:167
  74.1 31.0 %all_gather.33 = bf16[192,768]{0,1:T(8,128)(2,1)S(1)} all-gather(bf16[192,96]{0,1:T(8,128)(2,1)S(1)} %copy.36), channel_id=1, replica_groups=mesh['dp'=8,'tensor'=4] {'dp'}, dimensions={1}, use_global_device_ids=true | all-gather | bytes 331776 | tf_op jit(solution)/shard_map/all_gather | solution.py:168
  105.7 2.5 fusion.105
  110.7 12.7 %while.26 = (s32[]{:T(128)}, bf16[2,512,3,64]{1,3,2,0:T(8,128)(2,1)S(1)}, f32[2,3,512,1]{2,1,3,0:T(4,128)S(1)}, s32[2]{0:T(128)S(1)}, bf16[1152,3,64]{0,2,1:T(8,...) while((s32[]{:T(128)}, ...), condition=%wide.region_5.6_spmd, body=%wide.region_2.5_spmd.sunk | while | flops 264207360 | bytes 14069500 | solution.py:104
  114.8 2.3 fusion.144
  121.2 2.3 fusion.144
  124.7 2.8 convolution_convert_fusion.1
  128.3 30.0 %reduce-scatter.13.cloned.1.call-done = bf16[256,768]{1,0:T(8,128)(2,1)} async-done(((bf16[1024,768]{1,0:T(8,128)(2,1)}), bf16[256,768]{1,0:T(8,128)(2,1)}) %reduce-scatter.13.cloned.1.call-update) | async-done | bytes 393232 | tf_op jit(solution)/shard_map/reduce_scatter | solution.py:193
  162.0 31.1 %all_gather.37 = bf16[288,768]{0,1:T(8,128)(2,1)} all-gather(bf16[288,96]{0,1:T(8,128)(2,1)S(1)} %copy.38), channel_id=1, replica_groups=mesh['dp'=8,'tensor'=4] {'dp'}, dimensions={1}, use_global_device_ids=true | all-gather | bytes 497664 | tf_op jit(solution)/shard_map/all_gather | solution.py:170
  193.0 36.6 %all_gather.36 = bf16[768,2,288]{2,1,0:T(2,128)(2,1)} all-gather(bf16[96,2,288]{2,1,0:T(2,128)(2,1)S(1)} %copy-done.24), channel_id=1, replica_groups=mesh['dp'=8,'tensor'=4] {'dp'}, dimensions={0}, use_global_device_ids=true | all-gather | bytes 995328 | tf_op jit(solution)/shard_map/all_gather | solution.py:169
  231.9 2.9 fusion.48
  234.8 2.6 multiply_bitcast_fusion
  239.8 2.7 bitcast_convert_fusion.1
  246.1 27.2 %reduce-scatter.17.cloned.1.call-done = bf16[256,768]{1,0:T(8,128)(2,1)} async-done(((bf16[1024,768]{1,0:T(8,128)(2,1)}), bf16[256,768]{1,0:T(8,128)(2,1)}) %reduce-scatter.17.cloned.1.call-update) | async-done | bytes 393232 | tf_op jit(solution)/shard_map/reduce_scatter | solution.py:232
  275.4 28.5 %reduce-scatter.15.cloned.1.call-done = bf16[256,768]{1,0:T(8,128)(2,1)} async-done(((bf16[1024,768]{1,0:T(8,128)(2,1)}), bf16[256,768]{1,0:T(8,128)(2,1)}) %reduce-scatter.15.cloned.1.call-update) | async-done | bytes 393232 | tf_op jit(solution)/shard_map/reduce_scatter | solution.py:211
  308.0 3.6 convolution_bitcast_fusion
  312.8 4.7 fusion.46
  317.6 10.1 %all-gather.11.cloned.1.call-done = bf16[1024,768]{1,0:T(8,128)(2,1)} async-done(((bf16[256,768]{1,0:T(8,128)(2,1)}), bf16[1024,768]{1,0:T(8,128)(2,1)}) %all-gather.11.cloned.1.call-update) | async-done | bytes 1572880 | tf_op jit(solution)/shard_map/all_gather | solution.py:242
  327.7 3.3 convolution_bitcast_fusion.1
  333.4 35.1 %while.27 = (s32[]{:T(128)}, f32[1152,3,64]{0,2,1:T(8,128)S(1)}, f32[1152,3,64]{0,2,1:T(8,128)S(1)}, f32[2,512,3,64]{1,0,3,2:T(2,128)}, s32[2]{0:T(128)}, /*inde...) while((s32[]{:T(128)}, f32[1152,3,64]{0,2,1:T(8,128)S(1)}, ...), condition=%wide.region_15.16_spmd, body=%wide.region_13.15_spmd.sunk | while | flops 640097280 | bytes 35653420 | solution.py:150
  342.9 8.1 %dynamic_update_slice.31 = f32[2,512,3,64]{1,0,3,2:T(2,128)} dynamic-update-slice(f32[2,512,3,64]{1,0,3,2:T(2,128)} %get-tuple-element.438, f32[1,512,3,64]{1,0,3,2:T(1,128)S(1)} %copy.73, s32[]{:T(128)S(6)} %copy.94, s32[]{:T(128)} %constant.82.clone.1..sunk.1, s32[]{:T(128)} %constant.82.clone.1..sunk.1, s32[]{:T(128)} %constant.82.clone.1..sunk.1) | dynamic-update-slice | bytes 786436 | tf_op jit(solution)/shard_map/while/body/jit(dynamic_update_index_in_dim)/dynamic_update_slice | solution.py:150
  360.4 8.1 %dynamic_update_slice.31 = f32[2,512,3,64]{1,0,3,2:T(2,128)} dynamic-update-slice(f32[2,512,3,64]{1,0,3,2:T(2,128)} %get-tuple-element.438, f32[1,512,3,64]{1,0,3,2:T(1,128)S(1)} %copy.73, s32[]{:T(128)S(6)} %copy.94, s32[]{:T(128)} %constant.82.clone.1..sunk.1, s32[]{:T(128)} %constant.82.clone.1..sunk.1, s32[]{:T(128)} %constant.82.clone.1..sunk.1) | dynamic-update-slice | bytes 786436 | tf_op jit(solution)/shard_map/while/body/jit(dynamic_update_index_in_dim)/dynamic_update_slice | solution.py:150
  372.0 2.6 bitcast_convert_fusion
  375.6 4.3 fusion.44
  380.6 14.9 %reduce-scatter.27.cloned.1.call-done = f32[96,288]{1,0:T(8,128)} async-done(((f32[768,288]{1,0:T(8,128)}), f32[96,288]{1,0:T(8,128)}) %reduce-scatter.27.cloned.1.call-update) | async-done | bytes 110608
  397.2 69.9 %reduce-scatter.23.cloned.1.call-done = f32[96,2,288]{2,0,1:T(8,128)} async-done(((f32[768,2,288]{2,0,1:T(8,128)}), f32[96,2,288]{2,0,1:T(8,128)}) %reduce-scatter.23.cloned.1.call-update) | async-done | bytes 221200 | tf_op jit(solution)/shard_map/reduce_scatter | solution.py:278
  468.9 63.6 %reduce-scatter.25.cloned.1.call-done = f32[96,192]{1,0:T(8,128)} async-done(((f32[768,192]{1,0:T(8,128)}), f32[96,192]{1,0:T(8,128)}) %reduce-scatter.25.cloned.1.call-update) | async-done | bytes 73744
  534.1 28.3 %reduce-scatter.19.cloned.1.call-done = bf16[256,768]{1,0:T(8,128)(2,1)} async-done(((bf16[1024,768]{1,0:T(8,128)(2,1)}), bf16[256,768]{1,0:T(8,128)(2,1)}) %reduce-scatter.19.cloned.1.call-update) | async-done | bytes 393232 | tf_op jit(solution)/shard_map/reduce_scatter | solution.py:264
  565.3 19.0 %all-reduce.9 = (f32[768]{0:T(1024)S(1)}, f32[768]{0:T(1024)S(1)}) all-reduce(f32[768]{0:T(1024)S(1)} %get-tuple-element.151, f32[768]{0:T(1024)S(1)} %copy-done.31), channel_id=10, replica_groups=mesh['dp'=8,'tensor'=4] {'dp'}, use_global_device_ids=true, to_apply=%region_25.26.clone | all-reduce | flops 1536 | bytes 12288
  584.4 6.4 all-reduce.10
  591.9 43.5 %reduce-scatter.21.cloned.1.call-done = f32[96,3,192]{2,0,1:T(8,128)} async-done(((f32[768,3,192]{2,0,1:T(8,128)}), f32[96,3,192]{2,0,1:T(8,128)}) %reduce-scatter.21.cloned.1.call-update) | async-done | bytes 221200 | tf_op jit(solution)/shard_map/reduce_scatter | solution.py:276
  (208 shorter events, 75.6 us)
Async XLA Ops:
  7.2 27.2 %copy-start.26 = (bf16[192,96]{1,0:T(8,128)(2,1)S(1)}, bf16[192,96]{1,0:T(8,128)(2,1)}, u32[]{:S(2)}) copy-start(bf16[192,96]{1,0:T(8,128)(2,1)} %param.16) | copy-start | bytes 110596
  7.2 27.3 %copy-start.23 = (bf16[96,3,192]{2,0,1:T(8,128)(2,1)S(1)}, bf16[96,3,192]{2,0,1:T(8,128)(2,1)}, u32[]{:S(2)}) copy-start(bf16[96,3,192]{2,0,1:T(8,128)(2,1)} %param.15) | copy-start | bytes 331780
  7.2 98.5 %all-gather.5.cloned.1.call-start = ((), (), s32[]{:S(2)}) async-start(), calls=%async_computation.8 | async-start | bytes 1966080 | tf_op jit(solution)/shard_map/all_gather | solution.py:182
  8.4 25.9 %copy-start.27 = (f32[256]{0:T(256)}, f32[256]{0:T(256)S(1)}, u32[]{:S(2)}) copy-start(f32[256]{0:T(256)S(1)} %broadcast_multiply_fusion.1) | copy-start | bytes 3076
  9.7 24.7 %copy-start.32 = (f32[256]{0:T(256)}, f32[256]{0:T(256)S(1)}, u32[]{:S(2)}) copy-start(f32[256]{0:T(256)S(1)} %fusion.85) | copy-start | bytes 3076
  9.7 24.6 %copy-start.29 = (f32[256]{0:T(256)}, f32[256]{0:T(256)S(1)}, u32[]{:S(2)}) copy-start(f32[256]{0:T(256)S(1)} %fusion.95) | copy-start | bytes 3076
  34.2 124.0 %reduce-scatter.13.cloned.1.call-start = ((), (), s32[]{:S(2)}) async-start(), calls=%async_computation.9 | async-start | bytes 1966080 | tf_op jit(solution)/shard_map/reduce_scatter | solution.py:193
  70.7 37.5 %copy-start.16 = (bf16[768,3,192]{0,2,1:T(8,128)(2,1)}, bf16[768,3,192]{0,2,1:T(8,128)(2,1)S(1)}, u32[]{:S(2)}) copy-start(bf16[768,3,192]{0,2,1:T(8,128)(2,1)S(1)} %copy.34) | copy-start | bytes 2654212
  105.7 3.8 copy-start.12
  127.4 30.8 %copy-start = (bf16[256,768]{1,0:T(8,128)(2,1)S(1)}, bf16[256,768]{1,0:T(8,128)(2,1)}, u32[]{:S(2)}) copy-start(bf16[256,768]{1,0:T(8,128)(2,1)} %param.13) | copy-start | bytes 1179652
  127.5 102.2 %all-gather.9.cloned.1.call-start = ((), (), s32[]{:S(2)}) async-start(), calls=%async_computation.12 | async-start | bytes 1966080 | tf_op jit(solution)/shard_map/all_gather | solution.py:220
  128.2 103.7 %all-gather.7.cloned.1.call-start = ((), (), s32[]{:S(2)}) async-start(), calls=%async_computation.10 | async-start | bytes 1966080 | tf_op jit(solution)/shard_map/all_gather | solution.py:200
  160.8 32.2 %copy-start.24 = (bf16[96,2,288]{2,1,0:T(2,128)(2,1)S(1)}, bf16[96,2,288]{2,1,0:T(2,128)(2,1)}, u32[]{:S(2)}) copy-start(bf16[96,2,288]{2,1,0:T(2,128)(2,1)} %param.17) | copy-start | bytes 331780
  161.8 111.5 %reduce-scatter.17.cloned.1.call-start = ((), (), s32[]{:S(2)}) async-start(), calls=%async_computation.13 | async-start | bytes 1966080 | tf_op jit(solution)/shard_map/reduce_scatter | solution.py:232
  242.5 61.4 %reduce-scatter.15.cloned.1.call-start = ((), (), s32[]{:S(2)}) async-start(), calls=%async_computation.11 | async-start | bytes 1966080 | tf_op jit(solution)/shard_map/reduce_scatter | solution.py:211
  246.0 81.7 %all-gather.11.cloned.1.call-start = ((), (), s32[]{:S(2)}) async-start(), calls=%async_computation.14 | async-start | bytes 1966080 | tf_op jit(solution)/shard_map/all_gather | solution.py:242
  273.3 30.6 %copy-start.9 = (bf16[256,768]{1,0:T(8,128)(2,1)S(1)}, bf16[256,768]{1,0:T(8,128)(2,1)}, u32[]{:S(2)}) copy-start(bf16[256,768]{1,0:T(8,128)(2,1)} %reduce-scatter.17.cloned.1.call-done) | copy-start | bytes 1179652
  275.4 31.6 %copy-start.6 = (bf16[256,768]{1,0:T(8,128)(2,1)S(1)}, bf16[256,768]{1,0:T(8,128)(2,1)}, u32[]{:S(2)}) copy-start(bf16[256,768]{1,0:T(8,128)(2,1)} %param.21) | copy-start | bytes 1179652
  306.0 5.5 copy-start.34
  307.9 87.5 %reduce-scatter.27.cloned.1.call-start = ((), (), s32[]{:S(2)}) async-start(), calls=%async_computation.19 | async-start | bytes 1327104
  311.6 155.4 %reduce-scatter.23.cloned.1.call-start = ((), (), s32[]{:S(2)}) async-start(), calls=%async_computation.17 | async-start | bytes 2654208 | tf_op jit(solution)/shard_map/reduce_scatter | solution.py:278
  317.5 215.0 %reduce-scatter.25.cloned.1.call-start = ((), (), s32[]{:S(2)}) async-start(), calls=%async_computation.18 | async-start | bytes 884736
  331.0 231.4 %reduce-scatter.19.cloned.1.call-start = ((), (), s32[]{:S(2)}) async-start(), calls=%async_computation.15 | async-start | bytes 1966080 | tf_op jit(solution)/shard_map/reduce_scatter | solution.py:264
  374.6 260.8 %reduce-scatter.21.cloned.1.call-start = ((), (), s32[]{:S(2)}) async-start(), calls=%async_computation.16 | async-start | bytes 2654208 | tf_op jit(solution)/shard_map/reduce_scatter | solution.py:276
  379.9 182.5 %copy-start.28 = (f32[256]{0:T(256)S(1)}, f32[256]{0:T(256)}, u32[]{:S(2)}) copy-start(f32[256]{0:T(256)} %copy-done.27) | copy-start | bytes 3076
  379.9 183.9 %copy-start.33 = (f32[256]{0:T(256)S(1)}, f32[256]{0:T(256)}, u32[]{:S(2)}) copy-start(f32[256]{0:T(256)} %copy-done.32) | copy-start | bytes 3076
  379.9 183.9 %copy-start.30 = (f32[256]{0:T(256)S(1)}, f32[256]{0:T(256)}, u32[]{:S(2)}) copy-start(f32[256]{0:T(256)} %copy-done.29) | copy-start | bytes 3076
  397.1 168.1 %copy-start.31 = (f32[768]{0:T(1024)S(1)}, f32[768]{0:T(1024)}, u32[]{:S(2)}) copy-start(f32[768]{0:T(1024)} %get-tuple-element.149) | copy-start | bytes 9220
  397.1 193.6 %copy-start.3 = (f32[256,768]{1,0:T(8,128)S(1)}, f32[256,768]{1,0:T(8,128)}, u32[]{:S(2)}) copy-start(f32[256,768]{1,0:T(8,128)} %copy-done.2) | copy-start | bytes 2359300
  397.1 193.6 %copy-start.7 = (bf16[256,768]{1,0:T(8,128)(2,1)S(1)}, bf16[256,768]{1,0:T(8,128)(2,1)}, u32[]{:S(2)}) copy-start(bf16[256,768]{1,0:T(8,128)(2,1)} %param.21) | copy-start | bytes 1179652
  397.1 193.6 %copy-start.35 = (f32[256]{0:T(256)S(1)}, f32[256]{0:T(256)}, u32[]{:S(2)}) copy-start(f32[256]{0:T(256)} %copy-done.34) | copy-start | bytes 3076
  562.4 28.4 %copy-start.5 = (bf16[256,768]{1,0:T(8,128)(2,1)S(1)}, bf16[256,768]{1,0:T(8,128)(2,1)}, u32[]{:S(2)}) copy-start(bf16[256,768]{1,0:T(8,128)(2,1)} %reduce-scatter.19.cloned.1.call-done) | copy-start | bytes 1179652
  (17 other events, 26.7 us)
Sparse Core Ops, SparseCore 0:
  34.4 19.6 all-gather.4
  127.6 30.6 reduce-scatter.12
  159.9 19.6 all-gather.8
  181.7 19.6 all-gather.6
  242.6 30.5 reduce-scatter.16
  275.7 28.1 reduce-scatter.14
  308.0 19.6 all-gather.10
  331.5 63.9 reduce-scatter.26
  399.4 67.6 reduce-scatter.22
  470.5 61.9 reduce-scatter.24
  535.0 27.3 reduce-scatter.18
  566.7 68.6 reduce-scatter.20
where the time goes:
time: 647 us; the launch traced here: 642 us
  waiting for transfers between devices  317 us (49%)
  blocking collectives  178 us (28%)
  matrix products  53.9 us (8%)
  local copies, waits for them, and re-layouts  43.7 us (7%)
  other arithmetic  28.8 us (4%)
  between operations  17.4 us (3%)
    unnamed x14, waiting for transfers between devices  79.3 us
    reduce_scatter x1, waiting for transfers between devices, on_device(): lax.psum_scatter(grad_in_w, 'dp', scatter_dimension=0, tiled=True)  69.9 us
    reduce_scatter x1, waiting for transfers between devices, on_device(): lax.psum_scatter(grad_qkv_w, 'dp', scatter_dimension=0, tiled=True)  43.5 us
    unnamed x2, blocking collectives  37.8 us
    all_gather x1, blocking collectives, on_device(): lax.all_gather(w_in, 'dp', axis=0, tiled=True)  36.6 us
    all_gather x1, blocking collectives, on_device(): lax.all_gather(w_qkv, 'dp', axis=0, tiled=True)  35.2 us
    all_gather x1, blocking collectives, on_device(): lax.all_gather(w_mlp_out, 'dp', axis=1, tiled=True)  31.1 us
    all_gather x1, blocking collectives, on_device(): lax.all_gather(w_attn_out, 'dp', axis=1, tiled=True)  31 us
  transfers between devices with their start and end apart: 12, of which 9 were waited for; matrix products, arithmetic and copies ran while one was open for 12% of the time, Pallas kernels for 0%

commit v1 on v0

--- a/solution.py
+++ b/solution.py
@@ -1,21 +1,258 @@
+import functools
+
 import jax
 import jax.numpy as jnp
 from jax import lax
+from jax.experimental import pallas as pl
+from jax.experimental.pallas import tpu as pltpu
 from jax.sharding import PartitionSpec as P
 
 HEAD_DIM = 64
 WINDOW = 128
-
-
 NORM_EPS = 1e-05
 ROPE_BASE = 10000.0
 MASKED = -1e30
-
-
-def norm_rows(values, gain):
+MESH = pl.DeviceIdType.MESH
+BF = jnp.bfloat16
+F32 = jnp.float32
+NT = (((1,), (1,)), ((), ()))
+VMEM = pl.BlockSpec(memory_space=pltpu.VMEM)
+ANY = pl.BlockSpec(memory_space=pl.ANY)
+
+
+def normal_rows(values):
     centre = values - jnp.mean(values, axis=-1, keepdims=True)
     spread = jnp.mean(centre * centre, axis=-1, keepdims=True)
-    return centre * lax.rsqrt(spread + NORM_EPS) * gain
+    inv = lax.rsqrt(spread + NORM_EPS)
+    return centre * inv, inv
+
+
+def normal_back(values, grad):
+    xhat, inv = normal_rows(values)
+    mean_g = jnp.mean(grad, axis=-1, keepdims=True)
+    mean_gx = jnp.mean(grad * xhat, axis=-1, keepdims=True)
+    return inv * (grad - mean_g - xhat * mean_gx)
+
+
+def remote(src, dst, send, recv, dev):
+    return pltpu.make_async_remote_copy(
+        src_ref=src, dst_ref=dst, send_sem=send, recv_sem=recv, device_id=dev, device_id_type=MESH
+    )
+
+
+def tensor_place():
+    dp, t = lax.axis_index("dp"), lax.axis_index("tensor")
+    x, core = lax.div(t, 2), lax.rem(t, 2)
+    return dp, t, x, core, x * 2 + 1 - core, (1 - x) * 2 + core
+
+
+def dp_place(dp_size):
+    dp, t = lax.axis_index("dp"), lax.axis_index("tensor")
+    return dp, t, lax.div(dp, 2), lax.rem(dp, 2), dp_size // 2
+
+
+def greet(devices):
+    barrier = pltpu.get_barrier_semaphore()
+    for dev in devices:
+        pl.semaphore_signal(barrier, inc=1, device_id=dev, device_id_type=MESH)
+    pl.semaphore_wait(barrier, len(devices))
+
+
+def tensor_peers():
+    dp, t, x, core, corep, xp = tensor_place()
+    return [(dp, corep), (dp, xp)]
+
+
+def dp_peers(dp_size):
+    dp, t, hi, lo, high = dp_place(dp_size)
+    return [(hi * 2 + 1 - lo, t)] + [(lax.rem(hi + k, high) * 2 + lo, t) for k in range(1, high)]
+
+
+class Gather:
+    def __init__(self, src, out, sems):
+        dp, t, x, core, corep, xp = tensor_place()
+        send, recv, here = sems
+        self.own = pltpu.make_async_copy(src, out.at[t], here)
+        self.over_x = remote(src, out.at[t], send.at[0], recv.at[0], (dp, xp))
+        self.to_core = remote(src, out.at[t], send.at[1], recv.at[1], (dp, corep))
+        self.relay = remote(out.at[xp], out.at[xp], send.at[2], recv.at[2], (dp, corep))
+
+    def start(self):
+        self.over_x.start()
+        self.to_core.start()
+        self.own.start()
+
+    def forward(self):
+        self.over_x.wait_recv()
+        self.relay.start()
+
+    def finish(self):
+        self.to_core.wait_recv()
+        self.relay.wait_recv()
+        self.over_x.wait_send()
+        self.to_core.wait_send()
+        self.relay.wait_send()
+        self.own.wait()
+
+
+GATHER_SEMS = [pltpu.SemaphoreType.DMA((3,)), pltpu.SemaphoreType.DMA((3,)), pltpu.SemaphoreType.DMA]
+
+
+def scatter_sum(part, scratch):
+    sbuf, r1, pbuf, r2, send, recv = scratch
+    dp, t, x, core, corep, xp = tensor_place()
+    far = remote(sbuf.at[0], r1.at[0], send.at[0], recv.at[0], (dp, corep))
+    near = remote(sbuf.at[1], r1.at[1], send.at[1], recv.at[1], (dp, corep))
+    over = remote(pbuf, r2, send.at[2], recv.at[2], (dp, xp))
+    sbuf[0] = part((1 - x) * 2 + 1 - core).astype(BF)
+    far.start()
+    mine = part(xp)
+    far.wait_recv()
+    pbuf[...] = (mine + r1[0].astype(F32)).astype(BF)
+    over.start()
+    sbuf[1] = part(corep).astype(BF)
+    near.start()
+    total = part(t)
+    near.wait_recv()
+    total = total + r1[1].astype(F32)
+    over.wait_recv()
+    total = total + r2[...].astype(F32)
+    far.wait_send()
+    near.wait_send()
+    over.wait_send()
+    return total
+
+
+def scatter_scratch(rows, width):
+    return [
+        pltpu.VMEM((2, rows, width), BF),
+        pltpu.VMEM((2, rows, width), BF),
+        pltpu.VMEM((rows, width), BF),
+        pltpu.VMEM((rows, width), BF),
+        pltpu.SemaphoreType.DMA((3,)),
+        pltpu.SemaphoreType.DMA((3,)),
+    ]
+
+
+def params(ident):
+    return pltpu.CompilerParams(
+        collective_id=ident, has_side_effects=True, vmem_limit_bytes=48 * 1024 * 1024
+    )
+
+
+def first_kernel(dp_size, tok, cot, slab, xfull, cfull, wfull, xhat, *scr):
+    gx, gc = Gather(xhat, xfull, scr[0:3]), Gather(cot, cfull, scr[3:6])
+    zsend, zrecv, ysend, yrecv, here = scr[6:]
+    dp, t, hi, lo, high = dp_place(dp_size)
+    ypeer = (hi * 2 + 1 - lo, t)
+    greet(tensor_peers() + dp_peers(dp_size))
+    mine = pltpu.make_async_copy(slab, wfull.at[dp], here)
+    ycopies = [remote(slab, wfull.at[dp], ysend.at[0], yrecv.at[0], ypeer)]
+    zcopies = []
+    for k in range(1, high):
+        peer = (lax.rem(hi + k, high) * 2 + lo, t)
+        zcopies.append(remote(slab, wfull.at[dp], zsend.at[k], zrecv.at[k], peer))
+        block = lax.rem(hi - k + high, high) * 2 + lo
+        ycopies.append(remote(wfull.at[block], wfull.at[block], ysend.at[k], yrecv.at[k], ypeer))
+    ycopies[0].start()
+    for copy in zcopies:
+        copy.start()
+    mine.start()
+    xhat[...] = normal_rows(tok[...].astype(F32))[0].astype(BF)
+    gx.start()
+    gc.start()
+    gx.forward()
+    gc.forward()
+    for k in range(1, high):
+        zcopies[k - 1].wait_recv()
+        ycopies[k].start()
+    gx.finish()
+    gc.finish()
+    for copy in ycopies:
+        copy.wait_recv()
+    for copy in ycopies + zcopies:
+        copy.wait_send()
+    mine.wait()
+
+
+def hidden_kernel(att, wo, tok, hid, x2full, xhat, *scr):
+    rows = tok.shape[0]
+    greet(tensor_peers())
+
+    def part(b):
+        lhs = att[pl.ds(pl.multiple_of(b * rows, rows), rows), :]
+        return lax.dot_general(lhs, wo[...], NT, preferred_element_type=F32)
+
+    hidden = tok[...].astype(F32) + scatter_sum(part, scr[3:9])
+    hid[...] = hidden
+    xhat[...] = normal_rows(hidden)[0].astype(BF)
+    gather = Gather(xhat, x2full, scr[0:3])
+    gather.start()
+    gather.forward()
+    gather.finish()
+
+
+def middle_kernel(gated, wm, dmix, win, hid, cot, out, dhid, dbfull, dbr, *scr):
+    rows = hid.shape[0]
+    greet(tensor_peers())
+
+    def part_of(lhs_ref, w_ref):
+        def part(b):
+            lhs = lhs_ref[pl.ds(pl.multiple_of(b * rows, rows), rows), :]
+            return lax.dot_general(lhs, w_ref[...], NT, preferred_element_type=F32)
+
+        return part
+
+    grad = scatter_sum(part_of(dmix, win), scr[3:9])
+    d_hidden = cot[...].astype(F32) + normal_back(hid[...], grad)
+    dhid[...] = d_hidden
+    dbr[...] = d_hidden.astype(BF)
+    gather = Gather(dbr, dbfull, scr[0:3])
+    gather.start()
+    gather.forward()
+    out[...] = (hid[...] + scatter_sum(part_of(gated, wm), scr[9:15])).astype(BF)
+    gather.finish()
+
+
+def last_kernel(dp_size, dproj, wqkv, tok, dhid, grads, gtok, gsum, ry, zs, zr, *scr):
+    rows = tok.shape[0]
+    ysend, yrecv, zsend, zrecv = scr[6:]
+    dp, t, hi, lo, high = dp_place(dp_size)
+    ypeer = (hi * 2 + 1 - lo, t)
+    greet(tensor_peers() + dp_peers(dp_size))
+    ycopies = []
+    zcopies = []
+    order = list(range(1, high)) + [0]
+    for k in range(high):
+        block_hi = lax.rem(hi + k, high)
+        ycopies.append(
+            remote(grads.at[block_hi * 2 + 1 - lo], ry.at[k], ysend.at[k], yrecv.at[k], ypeer)
+        )
+        zcopies.append(
+            remote(zs.at[k], zr.at[k], zsend.at[k], zrecv.at[k], (block_hi * 2 + lo, t))
+        )
+    for k in order:
+        ycopies[k].start()
+
+    def part(b):
+        lhs = dproj[pl.ds(pl.multiple_of(b * rows, rows), rows), :]
+        return lax.dot_general(lhs, wqkv[...], NT, preferred_element_type=F32)
+
+    grad = scatter_sum(part, scr[0:6])
+    gtok[...] = (dhid[...] + normal_back(tok[...].astype(F32), grad)).astype(BF)
+    for k in range(1, high):
+        ycopies[k].wait_recv()
+        block = lax.rem(hi + k, high) * 2 + lo
+        zs[k] = (grads[block].astype(F32) + ry[k].astype(F32)).astype(BF)
+        zcopies[k].start()
+    ycopies[0].wait_recv()
+    total = grads[hi * 2 + lo].astype(F32) + ry[0].astype(F32)
+    for k in range(1, high):
+        zcopies[k].wait_recv()
+        total = total + zr[k].astype(F32)
+    gsum[...] = total
+    for copy in ycopies + zcopies[1:]:
+        copy.wait_send()
 
 
 def run_layout(seq_pair, slot_count):
@@ -158,137 +395,153 @@
     )
 
 
-def gated_unit(mixed_proj):
-    return jax.nn.gelu(mixed_proj[:, 0], approximate=False) * mixed_proj[:, 1]
+def attention_forward(xfull, wqkv, lengths, nq):
+    slots = xfull.shape[0]
+    heads = nq // HEAD_DIM
+    run_ids, position = run_layout(lengths[0], slots)
+    cos_tab, sin_tab = rope_tables(position, HEAD_DIM)
+    proj = jnp.dot(xfull, wqkv, preferred_element_type=F32).reshape(slots, 3, heads, HEAD_DIM)
+    query = rotate(proj[:, 0], cos_tab, sin_tab).astype(BF)
+    key = rotate(proj[:, 1], cos_tab, sin_tab).astype(BF)
+    value = proj[:, 2].astype(BF)
+    attended, log_totals = attend_forward(query, key, value, run_ids)
+    return (query, key, value, log_totals, run_ids, cos_tab, sin_tab), attended.reshape(slots, nq)
+
+
+def attention_backward(saved, d_attended, lengths, nq):
+    query, key, value, log_totals, run_ids, cos_tab, sin_tab = saved
+    slots = query.shape[0]
+    dq, dk, dv = attend_backward(
+        query, key, value, run_ids, log_totals, d_attended.reshape(query.shape)
+    )
+    d_proj = jnp.stack(
+        [unrotate(dq, cos_tab, sin_tab), unrotate(dk, cos_tab, sin_tab), dv], axis=1
+    )
+    return d_proj.astype(BF).reshape(slots, 3 * nq)
 
 
 def on_device(tokens, lengths, w_qkv, w_attn_out, w_in, w_mlp_out, gain_attn, gain_mlp, cotangent):
-    gathered = (
-        lax.all_gather(w_qkv, "dp", axis=0, tiled=True),
-        lax.all_gather(w_attn_out, "dp", axis=1, tiled=True),
-        lax.all_gather(w_in, "dp", axis=0, tiled=True),
-        lax.all_gather(w_mlp_out, "dp", axis=1, tiled=True),
-        lax.all_gather(gain_attn, "dp", axis=0, tiled=True),
-        lax.all_gather(gain_mlp, "dp", axis=0, tiled=True),
-    )
-    qkv_full, attn_out_full, in_full, mlp_out_full, gain_one, gain_two = gathered
-    row_count = tokens.shape[0]
-    slot_count = row_count * lax.axis_size("tensor")
-    heads_here = qkv_full.shape[2] // HEAD_DIM
-    run_ids, position = run_layout(lengths[0], slot_count)
-    cos_tab, sin_tab = rope_tables(position, HEAD_DIM)
-    tokens_f = tokens.astype(jnp.float32)
-    normed_one_f, pull_norm_one = jax.vjp(norm_rows, tokens_f, gain_one.astype(jnp.float32))
-    normed_one_full = lax.all_gather(
-        normed_one_f.astype(jnp.bfloat16), "tensor", axis=0, tiled=True
-    )
-    proj = jnp.einsum("rd,dtc->rtc", normed_one_full, qkv_full, preferred_element_type=jnp.float32)
-    proj = proj.reshape(slot_count, 3, heads_here, HEAD_DIM)
-    query_rot = rotate(proj[:, 0], cos_tab, sin_tab).astype(jnp.bfloat16)
-    key_rot = rotate(proj[:, 1], cos_tab, sin_tab).astype(jnp.bfloat16)
-    value_low = proj[:, 2].astype(jnp.bfloat16)
-    attended, log_totals = attend_forward(query_rot, key_rot, value_low, run_ids)
-    attended_flat = attended.reshape(slot_count, heads_here * HEAD_DIM)
-    rows_part = attended_flat
-    hidden = tokens_f + lax.psum_scatter(
-        jnp.dot(rows_part, attn_out_full, preferred_element_type=jnp.float32).astype(jnp.bfloat16),
-        "tensor",
-        scatter_dimension=0,
-        tiled=True,
-    ).astype(jnp.float32)
-    normed_two_f, pull_norm_two = jax.vjp(norm_rows, hidden, gain_two.astype(jnp.float32))
-    normed_two_full = lax.all_gather(
-        normed_two_f.astype(jnp.bfloat16), "tensor", axis=0, tiled=True
-    )
-    mixed_proj = jnp.einsum(
-        "rd,dtc->rtc", normed_two_full, in_full, preferred_element_type=jnp.float32
-    )
-    gated_f, pull_gate = jax.vjp(gated_unit, mixed_proj)
-    gated_act = gated_f.astype(jnp.bfloat16)
-    rows_part = gated_act
-    output = (
-        hidden
-        + lax.psum_scatter(
-            jnp.dot(rows_part, mlp_out_full, preferred_element_type=jnp.float32).astype(
-                jnp.bfloat16
-            ),
-            "tensor",
-            scatter_dimension=0,
-            tiled=True,
-        ).astype(jnp.float32)
-    ).astype(jnp.bfloat16)
-    grad_out_full = lax.all_gather(cotangent, "tensor", axis=0, tiled=True)
-    grad_gated = jnp.einsum(
-        "rd,fd->rf", grad_out_full, mlp_out_full, preferred_element_type=jnp.float32
-    )
-    grad_mlp_out_w = jnp.einsum(
-        "rf,rd->fd", gated_act, grad_out_full, preferred_element_type=jnp.float32
-    )
-    grad_mixed = pull_gate(grad_gated)[0].astype(jnp.bfloat16)
-    grad_in_w = jnp.einsum(
-        "rd,rtc->dtc", normed_two_full, grad_mixed, preferred_element_type=jnp.float32
-    )
-    rows_part = grad_mixed
-    grad_normed_two = lax.psum_scatter(
-        jnp.einsum("rtc,dtc->rd", rows_part, in_full, preferred_element_type=jnp.float32).astype(
-            jnp.bfloat16
+    dp_size, tensor_size = lax.axis_size("dp"), lax.axis_size("tensor")
+    rows, width = tokens.shape
+    own = w_qkv.shape[0]
+    slots = rows * tensor_size
+    nq, nf = w_qkv.shape[2], w_in.shape[2]
+    c_attn, c_in, c_mlp, c_all = 3 * nq, 4 * nq, 4 * nq + 2 * nf, 4 * nq + 3 * nf
+    gain_one = gain_attn.astype(F32)[:, None]
+    gain_two = gain_mlp.astype(F32)[:, None]
+    qkv_own = w_qkv.reshape(own, 3 * nq).astype(F32)
+    in_own = w_in.reshape(own, 2 * nf).astype(F32)
+    slab = jnp.concatenate(
+        [
+            (qkv_own * gain_one).astype(BF),
+            w_attn_out.T,
+            (in_own * gain_two).astype(BF),
+            w_mlp_out.T,
+        ],
+        axis=1,
+    )
+    full = jax.ShapeDtypeStruct((tensor_size, rows, width), BF)
+    half = dp_size // 2
+    xfull, cfull, wfull = pl.pallas_call(
+        functools.partial(first_kernel, dp_size),
+        out_shape=(full, full, jax.ShapeDtypeStruct((dp_size, own, c_all), BF)),
+        in_specs=[VMEM, VMEM, ANY],
+        out_specs=(ANY, ANY, ANY),
+        scratch_shapes=[pltpu.VMEM((rows, width), BF)]
+        + GATHER_SEMS * 2
+        + [pltpu.SemaphoreType.DMA((half,))] * 4
+        + [pltpu.SemaphoreType.DMA],
+        compiler_params=params(0),
+    )(tokens, cotangent, slab)
+    xfull = xfull.reshape(slots, width)
+    cfull = cfull.reshape(slots, width)
+    wfull = wfull.reshape(width, c_all)
+    wqkv, wo = wfull[:, :c_attn], wfull[:, c_attn:c_in]
+    win, wm = wfull[:, c_in:c_mlp], wfull[:, c_mlp:]
+
+    saved, attended = attention_forward(xfull, wqkv, lengths, nq)
+
+    hid, x2full = pl.pallas_call(
+        hidden_kernel,
+        out_shape=(jax.ShapeDtypeStruct((rows, width), F32), full),
+        in_specs=[VMEM] * 3,
+        out_specs=(VMEM, ANY),
+        scratch_shapes=[pltpu.VMEM((rows, width), BF)] + GATHER_SEMS + scatter_scratch(rows, width),
+        compiler_params=params(1),
+    )(attended, wo, tokens)
+    x2full = x2full.reshape(slots, width)
+
+    mixed = jnp.dot(x2full, win, preferred_element_type=F32)
+    d_gated = jnp.dot(cfull, wm, preferred_element_type=F32)
+
+    def gate(inputs, gates):
+        return jax.nn.gelu(inputs, approximate=False) * gates
+
+    gated_f, pull = jax.vjp(gate, mixed[:, :nf], mixed[:, nf:])
+    gated = gated_f.astype(BF)
+    d_mixed = jnp.concatenate(pull(d_gated), axis=1).astype(BF)
+
+    output, dhid, dbfull = pl.pallas_call(
+        middle_kernel,
+        out_shape=(
+            jax.ShapeDtypeStruct((rows, width), BF),
+            jax.ShapeDtypeStruct((rows, width), F32),
+            full,
         ),
-        "tensor",
-        scatter_dimension=0,
-        tiled=True,
-    ).astype(jnp.float32)
-    grad_hidden_part, grad_gain_two = pull_norm_two(grad_normed_two)
-    grad_hidden = cotangent.astype(jnp.float32) + grad_hidden_part
-    grad_branch_full = lax.all_gather(
-        grad_hidden.astype(jnp.bfloat16), "tensor", axis=0, tiled=True
-    )
-    grad_attn_out_w = jnp.einsum(
-        "rc,rd->cd", attended_flat, grad_branch_full, preferred_element_type=jnp.float32
-    )
-    grad_attended = jnp.einsum(
-        "rd,cd->rc", grad_branch_full, attn_out_full, preferred_element_type=jnp.float32
-    )
-    grad_attended = grad_attended.astype(jnp.bfloat16).reshape(slot_count, heads_here, HEAD_DIM)
-    grad_query, grad_key, grad_value = attend_backward(
-        query_rot, key_rot, value_low, run_ids, log_totals, grad_attended
-    )
-    grad_proj = jnp.stack(
-        [unrotate(grad_query, cos_tab, sin_tab), unrotate(grad_key, cos_tab, sin_tab), grad_value],
+        in_specs=[VMEM] * 6,
+        out_specs=(VMEM, VMEM, ANY),
+        scratch_shapes=[pltpu.VMEM((rows, width), BF)]
+        + GATHER_SEMS
+        + scatter_scratch(rows, width) * 2,
+        compiler_params=params(2),
+    )(gated, wm, d_mixed, win, hid, cotangent)
+    dbfull = dbfull.reshape(slots, width)
+
+    d_attended = jnp.dot(dbfull, wo, preferred_element_type=F32).astype(BF)
+    d_proj = attention_backward(saved, d_attended, lengths, nq)
+
+    def over_rows(left, right):
+        return lax.dot_general(
+            left, right, (((0,), (0,)), ((), ())), preferred_element_type=F32
+        ).astype(BF)
+
+    grads = jnp.concatenate(
+        [
+            over_rows(xfull, d_proj),
+            over_rows(dbfull, attended),
+            over_rows(x2full, d_mixed),
+            over_rows(cfull, gated),
+        ],
         axis=1,
-    )
-    grad_proj = grad_proj.astype(jnp.bfloat16).reshape(slot_count, 3, heads_here * HEAD_DIM)
-    grad_qkv_w = jnp.einsum(
-        "rd,rtc->dtc", normed_one_full, grad_proj, preferred_element_type=jnp.float32
-    )
-    rows_part = grad_proj
-    grad_normed_one = lax.psum_scatter(
-        jnp.einsum("rtc,dtc->rd", rows_part, qkv_full, preferred_element_type=jnp.float32).astype(
-            jnp.bfloat16
+    ).reshape(dp_size, own, c_all)
+    block = pltpu.VMEM((half, own, c_all), BF)
+    grad_tokens, gsum = pl.pallas_call(
+        functools.partial(last_kernel, dp_size),
+        out_shape=(
+            jax.ShapeDtypeStruct((rows, width), BF),
+            jax.ShapeDtypeStruct((own, c_all), F32),
         ),
-        "tensor",
-        scatter_dimension=0,
-        tiled=True,
-    ).astype(jnp.float32)
-    grad_rows_part, grad_gain_one = pull_norm_one(grad_normed_one)
-    grad_tokens = (grad_hidden + grad_rows_part).astype(jnp.bfloat16)
-    gain_sums = lax.psum((grad_gain_one, grad_gain_two), "tensor")
-    results = (
-        lax.psum_scatter(grad_qkv_w, "dp", scatter_dimension=0, tiled=True),
-        lax.psum_scatter(grad_attn_out_w, "dp", scatter_dimension=1, tiled=True),
-        lax.psum_scatter(grad_in_w, "dp", scatter_dimension=0, tiled=True),
-        lax.psum_scatter(grad_mlp_out_w, "dp", scatter_dimension=1, tiled=True),
-        lax.psum_scatter(gain_sums[0], "dp", scatter_dimension=0, tiled=True),
-        lax.psum_scatter(gain_sums[1], "dp", scatter_dimension=0, tiled=True),
+        in_specs=[VMEM] * 5,
+        out_specs=(VMEM, VMEM),
+        scratch_shapes=[block] * 3
+        + scatter_scratch(rows, width)
+        + [pltpu.SemaphoreType.DMA((half,))] * 4,
+        compiler_params=params(3),
+    )(d_proj, wqkv, tokens, dhid, grads)
+
+    sum_qkv, sum_in = gsum[:, :c_attn], gsum[:, c_in:c_mlp]
+    gain_grads = lax.psum(
+        jnp.stack([jnp.sum(sum_qkv * qkv_own, axis=1), jnp.sum(sum_in * in_own, axis=1)]), "tensor"
     )
     return (
         output,
         grad_tokens,
-        results[0],
-        results[1],
-        results[2],
-        results[3],
-        results[4],
-        results[5],
+        (sum_qkv * gain_one).reshape(own, 3, nq),
+        gsum[:, c_attn:c_in].T,
+        (sum_in * gain_two).reshape(own, 2, nf),
+        gsum[:, c_mlp:].T,
+        gain_grads[0],
+        gain_grads[1],
     )
 
 

time: 647 us -> 290 us (0.45)
  waiting for transfers between devices: 317 us -> 0 us
  blocking collectives: 178 us -> 7 us
  Pallas kernels: 0 us -> 157 us
  local copies, waits for them, and re-layouts: 43.7 us -> 63.5 us
  other arithmetic: 28.8 us -> 12.1 us
  between operations: 17.4 us -> 2.45 us
  matrix products: 53.9 us -> 42.9 us
    reduce_scatter x6 -> x0, waiting for transfers between devices: 227 us -> none  [the longest x1 69.9 us: on_device(): lax.psum_scatter(grad_in_w, 'dp', scatter_dimension=0, tiled=True)]
    pallas_call x0 -> x4, Pallas kernels: none -> 157 us  [the longest x1 50.1 us: on_device(): pl.pallas_call(functools.partial(last_kernel, dp_size), out_shape=(jax.Sh...]
    all_gather x4 -> x0, blocking collectives: 134 us -> none  [the longest x1 36.6 us: on_device(): lax.all_gather(w_in, 'dp', axis=0, tiled=True)]
    unnamed x14 -> x0, waiting for transfers between devices: 79.3 us -> none
    unnamed x2 -> x0, blocking collectives: 37.8 us -> none
    reduce_sum x8 -> x1, other arithmetic: 12 us -> 0.17 us  [on_device(): jnp.sum(sum_qkv * qkv_own, axis=1)]
    all_gather x4 -> x0, waiting for transfers between devices: 10.2 us -> none  [the longest x1 10.1 us: on_device(): lax.all_gather(grad_hidden.astype(jnp.bfloat16), 'tensor', axis=0, tiled=...]
    unnamed x3 -> x0, matrix products: 9.38 us -> none
  transfers between devices with their start and end apart: 12 -> 0, of which waited for: 9 -> 0; matrix products, arithmetic and copies ran while one was open for 12% -> 0% of each run, Pallas kernels for 0% -> 0%
where the time goes in v1:
time: 290 us; the launch traced here: 288 us
  Pallas kernels  157 us (54%)
  local copies, waits for them, and re-layouts  63.5 us (22%)
  matrix products  42.9 us (15%)
  other arithmetic  12.1 us (4%)
  blocking collectives  7 us (2%)
    pallas_call x1, Pallas kernels, on_device(): pl.pallas_call(functools.partial(last_kernel, dp_size), out_shape=(jax.Sh...  50.1 us
    pallas_call x1, Pallas kernels, on_device(): pl.pallas_call(functools.partial(first_kernel, dp_size), out_shape=(full,...  44.1 us
    pallas_call x1, Pallas kernels, on_device(): pl.pallas_call(middle_kernel, out_shape=(jax.ShapeDtypeStruct((rows, widt...  37.6 us
    pallas_call x1, Pallas kernels, on_device(): pl.pallas_call(hidden_kernel, out_shape=(jax.ShapeDtypeStruct((rows, widt...  25.3 us
    dynamic_update_slice x4, local copies, waits for them, and re-layouts, attend_backward(): lax.scan(one_block, (zero_grads, zero_grads), (block_ids, log_totals))  17 us
    unnamed x68, local copies, waits for them, and re-layouts  12.4 us
    dot_general x4, matrix products, block_scores(): jnp.einsum('ihc,jhc->hij', q_blk, k_blk, preferred_element_type=jnp.float32)  7.28 us
    psum x1, blocking collectives, on_device(): lax.psum(jnp.stack([jnp.sum(sum_qkv * qkv_own, axis=1), jnp.sum(sum_in *...  7 us

profile of v1, /device:TPU:8, one launch (start us, length us, event | category | flops | bytes accessed | tf_op | source)
XLA Modules:
  0.0 287.9 jit_solution(13948913846799930150)
XLA Ops:
  11.1 44.1 %shard_map.152 = (bf16[4,256,768]{2,1,0:T(8,128)(2,1)S(1)}, bf16[4,256,768]{2,1,0:T(8,128)(2,1)S(1)}, bf16[8,96,1632]{2,1,0:T(8,128)(2,1)}) custom-call(bf16[256,768]{1,0:T(8,128)(2,1)S(1)} %copy-done, bf16[256,768]{1,0:T(8,128)(2,1)S(1)} %copy-done.2, bf16[96,1632]{1,0:T(8,128)(2,1)S(1)} %concatenate.24.slab), custom_call_target="tpu_custom_call" | custom-call | tf_op jit(solution)/shard_map/pallas_call | solution.py:445
  55.3 2.5 slice.119.wo
  59.1 2.7 fusion.62
  61.8 2.2 copy.36
  64.0 2.7 fusion.64
  69.2 16.1 %while.26 = (s32[]{:T(128)}, bf16[2,512,3,64]{1,3,2,0:T(8,128)(2,1)}, f32[2,3,512,1]{2,1,3,0:T(4,128)S(1)}, s32[2]{0:T(128)S(1)}, bf16[1152,3,64]{0,2,1:T(8,128)...) while((s32[]{:T(128)}, ...), condition=%wide.region_3.4_spmd, body=%wide.region_0.3_spmd.sunk | while | flops 264207360 | bytes 17215284 | solution.py:341
  71.1 2.0 fusion.99
  74.2 2.3 fusion.100
  79.2 2.0 fusion.99
  82.3 2.3 fusion.100
  87.5 2.0 copy.38.att
  91.6 25.3 %shard_map.153 = (f32[256,768]{1,0:T(8,128)S(1)}, bf16[4,256,768]{2,1,0:T(8,128)(2,1)S(1)}) custom-call(bf16[1024,192]{1,0:T(8,128)(2,1)S(1)} %copy-done.1, bf16[768,192]{1,0:T(8,128)(2,1)S(1)} %copy-done.4, bf16[256,768]{1,0:T(8,128)(2,1)S(1)} %copy-done), custom_call_target="tpu_custom_call" | custom-call | tf_op jit(solution)/shard_map/pallas_call | solution.py:464
  116.9 2.7 fusion.59
  119.6 5.5 %add_convert_fusion = (bf16[1024,288]{1,0:T(8,128)(2,1)S(1)}, f32[1024,288]{1,0:T(8,128)S(1)}, f32[1024,288]{1,0:T(8,128)S(1)}) fusion(f32[1024,576]{1,0:T(8,128)S(1)} %fusion.59, bf16[1024,768]{1,0:T(8,128)(2,1)S(1)} %bitcast.115, bf16[768,1632]{1,0:T(8,128)(2,1)} %bitcast.128), kind=kOutput, calls=%fused_computation.58 | convolution fusion | flops 474513408 | bytes 7471104 | tf_op jit(solution)/shard_map/dot_general | solution.py:475
  127.5 2.1 convolution_convert_fusion.1
  129.5 37.6 %shard_map.154 = (bf16[256,768]{1,0:T(8,128)(2,1)S(1)}, f32[256,768]{1,0:T(8,128)S(1)}, bf16[4,256,768]{2,1,0:T(8,128)(2,1)}) custom-call(bf16[1024,288]{1,0:T(8,128)(2,1)S(1)} %get-tuple-element.214.gated, bf16[768,288]{1,0:T(8,128)(2,1)S(1)} %slice.123.wm, bf16[1024,576]{1,0:T(8,128)(2,1)S(1)} %pad_maximum_fusion.1.dmix, ...), custom_call_target="tpu_custom_call" | custom-call | tf_op jit(solution)/shard_map/pallas_call | solution.py:484
  167.2 3.5 %convolution_convert_fusion.3 = bf16[1024,192]{0,1:T(8,128)(2,1)} fusion(bf16[1024,768]{1,0:T(8,128)(2,1)} %bitcast.120, bf16[768,1632]{1,0:T(8,128)(2,1)} %bitcast.129), kind=kOutput, calls=%fused_computation.81 | convolution fusion | flops 302186496 | bytes 2359296 | tf_op jit(solution)/shard_map/dot_general | solution.py:500
  173.0 35.9 %while.27 = (s32[]{:T(128)}, f32[1152,3,64]{0,2,1:T(8,128)S(1)}, f32[1152,3,64]{0,2,1:T(8,128)}, f32[2,512,3,64]{1,0,3,2:T(2,128)}, s32[2]{0:T(128)S(1)}, /*inde...) while((s32[]{:T(128)}, f32[1152,3,64]{0,2,1:T(8,128)S(1)}, ...), condition=%wide.region_6.7_spmd, body=%wide.region_4.6_spmd.sunk | while | flops 640097280 | bytes 35653420 | solution.py:387
  174.9 1.8 fusion.109
  176.7 1.7 multiply_reduce_fusion.4
  178.8 2.5 fusion.112
  182.9 8.1 %dynamic_update_slice.31 = f32[2,512,3,64]{1,0,3,2:T(2,128)} dynamic-update-slice(f32[2,512,3,64]{1,0,3,2:T(2,128)} %get-tuple-element.447, f32[1,512,3,64]{1,0,3,2:T(1,128)S(1)} %copy.60, s32[]{:T(128)S(6)} %copy.79, s32[]{:T(128)} %constant.79.clone.1..sunk.1, s32[]{:T(128)} %constant.79.clone.1..sunk.1, s32[]{:T(128)} %constant.79.clone.1..sunk.1) | dynamic-update-slice | bytes 786436 | tf_op jit(solution)/shard_map/while/body/jit(dynamic_update_index_in_dim)/dynamic_update_slice | solution.py:387
  192.8 1.8 fusion.109
  194.6 1.7 multiply_reduce_fusion.4
  196.7 2.5 fusion.112
  200.8 8.1 %dynamic_update_slice.31 = f32[2,512,3,64]{1,0,3,2:T(2,128)} dynamic-update-slice(f32[2,512,3,64]{1,0,3,2:T(2,128)} %get-tuple-element.447, f32[1,512,3,64]{1,0,3,2:T(1,128)S(1)} %copy.60, s32[]{:T(128)S(6)} %copy.79, s32[]{:T(128)} %constant.79.clone.1..sunk.1, s32[]{:T(128)} %constant.79.clone.1..sunk.1, s32[]{:T(128)} %constant.79.clone.1..sunk.1) | dynamic-update-slice | bytes 786436 | tf_op jit(solution)/shard_map/while/body/jit(dynamic_update_index_in_dim)/dynamic_update_slice | solution.py:387
  208.9 1.9 reshape.286
  215.1 1.6 pad_maximum_fusion
  216.8 4.5 %copy.44 = bf16[768,1632]{1,0:T(8,128)(2,1)} copy(bf16[768,1632]{0,1:T(8,128)(2,1)} %pad_maximum_fusion) | data formatting | bytes 5013504 | tf_op jit(solution)/shard_map/concatenate | solution.py:508
  221.3 1.7 copy.45.dproj
  224.1 50.1 %shard_map.155 = (bf16[256,768]{1,0:T(8,128)(2,1)S(1)}, f32[96,1632]{1,0:T(8,128)S(1)}) custom-call(bf16[1024,576]{1,0:T(8,128)(2,1)S(1)} %copy.45.dproj, bf16[768,576]{1,0:T(8,128)(2,1)S(1)} %get-tuple-element.215.wqkv, bf16[256,768]{1,0:T(8,128)(2,1)S(1)} %copy-done, f32[256,768]{1,0:T(8,128)S(1)} %copy-done.6, bf16[8,96,1632]{2,1,0:T(8,128)(2,1)} %bitcast.119), custom_call_target="tpu_custom_call" | custom-call | tf_op jit(solution)/shard_map/pallas_call | solution.py:518
  275.2 7.0 %psum.7 = f32[2,96]{1,0:T(2,128)S(1)} all-reduce(f32[2,96]{1,0:T(2,128)S(1)} %pad_maximum_fusion.3), channel_id=1, replica_groups=mesh['dp'=8,'tensor'=4] {'tensor'}, use_global_device_ids=true, to_apply=%region_9.10 | all-reduce | flops 192 | bytes 1536 | tf_op jit(solution)/shard_map/psum | solution.py:533
  (154 shorter events, 46.5 us)
Async XLA Ops:
  7.2 3.9 %copy-start = (bf16[256,768]{1,0:T(8,128)(2,1)S(1)}, bf16[256,768]{1,0:T(8,128)(2,1)}, u32[]{:S(2)}) copy-start(bf16[256,768]{1,0:T(8,128)(2,1)} %tok.5) | copy-start | bytes 1179652
  7.2 3.9 %copy-start.2 = (bf16[256,768]{1,0:T(8,128)(2,1)S(1)}, bf16[256,768]{1,0:T(8,128)(2,1)}, u32[]{:S(2)}) copy-start(bf16[256,768]{1,0:T(8,128)(2,1)} %cot.3) | copy-start | bytes 1179652
  8.3 2.0 copy-start.19
  8.9 58.1 %copy-start.24 = (f32[1024,32]{0,1:T(8,128)}, f32[1024,32]{0,1:T(8,128)S(1)}, u32[]{:S(2)}) copy-start(f32[1024,32]{0,1:T(8,128)S(1)} %get-tuple-element.234) | copy-start | bytes 393220
  8.9 58.1 %copy-start.26 = (f32[1024,32]{0,1:T(8,128)}, f32[1024,32]{0,1:T(8,128)S(1)}, u32[]{:S(2)}) copy-start(f32[1024,32]{0,1:T(8,128)S(1)} %get-tuple-element.235) | copy-start | bytes 393220
  55.3 6.5 %copy-start.11 = (bf16[4,256,768]{2,1,0:T(8,128)(2,1)}, bf16[4,256,768]{2,1,0:T(8,128)(2,1)S(1)}, u32[]{:S(2)}) copy-start(bf16[4,256,768]{2,1,0:T(8,128)(2,1)S(1)} %get-tuple-element.130) | copy-start | bytes 4718596
  55.3 6.5 %copy-start.13 = (bf16[4,256,768]{2,1,0:T(8,128)(2,1)}, bf16[4,256,768]{2,1,0:T(8,128)(2,1)S(1)}, u32[]{:S(2)}) copy-start(bf16[4,256,768]{2,1,0:T(8,128)(2,1)S(1)} %get-tuple-element.134) | copy-start | bytes 4718596
  73.1 1.1 copy-start.30
  76.5 0.7 copy-start.31
  81.1 1.1 copy-start.30
  89.5 1.0 copy-start.1
  90.6 1.0 copy-start.4
  116.9 2.7 copy-start.14
  127.5 2.1 copy-start.3
  167.1 4.8 %copy-start.5 = (f32[256,768]{1,0:T(8,128)}, f32[256,768]{1,0:T(8,128)S(1)}, u32[]{:S(2)}) copy-start(f32[256,768]{1,0:T(8,128)S(1)} %get-tuple-element.142.dhid) | copy-start | bytes 2359300
  167.1 4.8 %copy-start.7 = (bf16[256,768]{1,0:T(8,128)(2,1)}, bf16[256,768]{1,0:T(8,128)(2,1)S(1)}, u32[]{:S(2)}) copy-start(bf16[256,768]{1,0:T(8,128)(2,1)S(1)} %get-tuple-element.486) | copy-start | bytes 1179652
  167.1 3.6 %copy-start.16 = (bf16[4,256,768]{2,1,0:T(8,128)(2,1)S(1)}, bf16[4,256,768]{2,1,0:T(8,128)(2,1)}, u32[]{:S(2)}) copy-start(bf16[4,256,768]{2,1,0:T(8,128)(2,1)} %get-tuple-element.138) | copy-start | bytes 4718596
  167.1 3.6 %copy-start.18 = (bf16[24,8,2,512]{3,1,2,0:T(8,128)(2,1)S(1)}, bf16[24,8,2,512]{3,1,2,0:T(8,128)(2,1)}, u32[]{:S(2)}) copy-start(bf16[24,8,2,512]{3,1,2,0:T(8,128)(2,1)} %copy.58) | copy-start | bytes 1179652
  170.7 2.3 copy-start.15
  208.9 1.9 copy-start.25
  208.9 1.9 copy-start.27
  211.1 2.7 copy-start.12
  212.7 1.1 copy-start.17
  213.8 1.1 copy-start.23
  213.8 1.3 copy-start.28
  213.8 1.4 copy-start.29
  223.0 1.1 copy-start.6
  224.1 50.9 %copy-start.20 = (f32[96,576]{1,0:T(8,128)S(1)}, f32[96,576]{1,0:T(8,128)}, u32[]{:S(2)}) copy-start(f32[96,576]{1,0:T(8,128)} %copy-done.19) | copy-start | bytes 663556
  224.1 50.9 %copy-start.22 = (f32[96,576]{1,0:T(8,128)S(1)}, f32[96,576]{1,0:T(8,128)}, u32[]{:S(2)}) copy-start(f32[96,576]{1,0:T(8,128)} %copy-done.21) | copy-start | bytes 663556
  274.3 0.7 copy-start.9
  275.2 11.2 %copy-start.8 = (bf16[256,768]{1,0:T(8,128)(2,1)S(1)}, bf16[256,768]{1,0:T(8,128)(2,1)}, u32[]{:S(2)}) copy-start(bf16[256,768]{1,0:T(8,128)(2,1)} %copy-done.7) | copy-start | bytes 1179652
  282.8 4.4 %copy-start.10 = (bf16[256,768]{1,0:T(8,128)(2,1)S(1)}, bf16[256,768]{1,0:T(8,128)(2,1)}, u32[]{:S(2)}) copy-start(bf16[256,768]{1,0:T(8,128)(2,1)} %copy-done.9) | copy-start | bytes 1179652
  (2 other events, 1.4 us)
